TPU v7x, 512 devices: a whole 4x8x8 slice. The times are simulated.
512 devices in a mesh: prompt: 16 (over y_lo, x, core), reply: 32 (over y_hi, z).
Axes of the slice: x: 4, y: 8 (y_hi: 4, y_lo: 2; y = y_hi * 2 + y_lo), z: 8, core: 2. Of those that a mesh axis runs over, the one named last changes fastest.
Arguments:
- q_prompt: bfloat16 [1024, 4096], P('prompt', 'reply'), may hold values from -6 to 6
- do_prompt: bfloat16 [1024, 4096], P('prompt', 'reply'), may hold values from -6 to 6
- kv_prompt: bfloat16 [2, 1024, 512], P(None, 'prompt'), may hold values from -6 to 6
- lse_prompt: float32 [32, 1024], P('reply', 'prompt')
- delta_prompt: float32 [32, 1024], P('reply', 'prompt'), may hold values from -8 to 8
- q_reply: bfloat16 [32, 1024, 4096], P('reply', 'prompt'), may hold values from -6 to 6
- do_reply: bfloat16 [32, 1024, 4096], P('reply', 'prompt'), may hold values from -6 to 6
- kv_reply: bfloat16 [2, 32, 1024, 512], P(None, 'reply', 'prompt'), may hold values from -6 to 6
- lse_reply: float32 [32, 32, 1024], P('reply', None, 'prompt')
- delta_reply: float32 [32, 32, 1024], P('reply', None, 'prompt'), may hold values from -8 to 8
- reply_len: int32 [32], P('reply'), may hold values from 256 to 1024, as said below
- reply_mask: int32 [32, 1024], P('reply', 'prompt'), may hold values 0 or 1
Outputs:
- dq_prompt: bfloat16 [1024, 4096], P('prompt', 'reply')
- dkv_prompt: bfloat16 [2, 1024, 512], P(None, 'prompt')
- dq_reply: bfloat16 [32, 1024, 4096], P('reply', 'prompt')
- dkv_reply: bfloat16 [2, 32, 1024, 512], P(None, 'reply', 'prompt')
Inputs may be any that keep to these rules, and one draw needn't show every extreme that they name: `reply_len`: at least one reply fills all 1024 positions.
All inputs are finite; a program needn't handle non-finite values. No bound on the sum of `reply_mask` on one device may be relied on, other than what follows from the above.
Results may differ from a plain program's by a relative error of at most 0.005.
Values may be sent and summed in bfloat16 or wider, within the bound.
A program may use at most 64 MiB of HBM per device.

v0:
```python
import jax
import jax.numpy as jnp
from jax import lax
from jax.sharding import PartitionSpec as P

H = 32
G = 4
DH = 128


def from_behind(block, axis, distance):
    devices = range(lax.axis_size(axis))
    route = [((i - distance) % len(devices), i) for i in devices]
    return lax.ppermute(block, axis, route)


def attend(q, do, lse, delta, k, v, allow):
    f = jnp.float32
    scale = q.shape[-1] ** (-0.5)
    score = jnp.einsum("qgxd,kgd->gxqk", q, k, preferred_element_type=f) * scale
    prob = jnp.where(allow, jnp.exp(score - lse[..., None]), 0.0)
    prob_b = prob.astype(jnp.bfloat16)
    dprob = jnp.einsum("qgxd,kgd->gxqk", do, v, preferred_element_type=f)
    dscore_b = (prob * (dprob - delta[..., None])).astype(jnp.bfloat16)
    grad_q = jnp.einsum("gxqk,kgd->qgxd", dscore_b, k, preferred_element_type=f) * scale
    grad_k = jnp.einsum("gxqk,qgxd->kgd", dscore_b, q, preferred_element_type=f) * scale
    grad_v = jnp.einsum("gxqk,qgxd->kgd", prob_b, do, preferred_element_type=f)
    return (grad_q, grad_k, grad_v)


def local(
    q_prompt,
    do_prompt,
    kv_prompt,
    lse_prompt,
    delta_prompt,
    q_reply,
    do_reply,
    kv_reply,
    lse_reply,
    delta_reply,
    reply_len,
    reply_mask,
):
    nprompt = lax.axis_size("prompt")
    mine = lax.axis_index("prompt")
    column = lax.axis_index("reply")
    pblock = kv_prompt.shape[1]
    kwidth = kv_prompt.shape[2]
    rblock = kv_reply.shape[2]
    qwidth = q_prompt.shape[1]
    heads_here = qwidth // DH
    group_size = H // G
    group = column * heads_here // group_size
    q_head = q_prompt.reshape(pblock, 1, heads_here, DH)
    do_head = do_prompt.reshape(pblock, 1, heads_here, DH)
    lse_head = lse_prompt.reshape(1, heads_here, pblock)
    delta_head = delta_prompt.reshape(1, heads_here, pblock)
    q_rows = q_reply.reshape(rblock, G, group_size, DH)
    do_rows = do_reply.reshape(rblock, G, group_size, DH)
    lse_rows = lse_reply.reshape(G, group_size, rblock)
    delta_rows = delta_reply.reshape(G, group_size, rblock)
    length = reply_len[0]
    qpos_p = mine * pblock + jnp.arange(pblock, dtype=jnp.int32)
    qpos_r = mine * rblock + jnp.arange(rblock, dtype=jnp.int32)
    qlive = qpos_r < length
    start = group * DH

    def turn_terms(step, kvp, kvr, maskr):
        source = (mine - step) % nprompt
        kpos_p = source * pblock + jnp.arange(pblock, dtype=jnp.int32)
        kpos_r = source * rblock + jnp.arange(rblock, dtype=jnp.int32)
        kgroup = lax.dynamic_slice_in_dim(kvp, start, DH, 2)

        def prompt_block():
            allow = kpos_p[None, :] <= qpos_p[:, None]
            return attend(
                q_head,
                do_head,
                lse_head,
                delta_head,
                kgroup[0][:, None, :],
                kgroup[1][:, None, :],
                allow,
            )

        def prompt_skip():
            return (
                jnp.zeros((pblock, 1, heads_here, DH), jnp.float32),
                jnp.zeros((pblock, 1, DH), jnp.float32),
                jnp.zeros((pblock, 1, DH), jnp.float32),
            )

        dq_one, dk_one, dv_one = lax.cond(source <= mine, prompt_block, prompt_skip)
        kvp_heads = kvp.reshape(2, pblock, G, DH)
        allow_all = jnp.broadcast_to(qlive[:, None], (rblock, pblock))
        dq_two, dk_two, dv_two = attend(
            q_rows, do_rows, lse_rows, delta_rows, kvp_heads[0], kvp_heads[1], allow_all
        )
        kvr_heads = kvr.reshape(2, rblock, G, DH)

        def reply_block():
            allow = (
                (kpos_r[None, :] <= qpos_r[:, None])
                & (kpos_r < length)[None, :]
                & (maskr > 0.5)[None, :]
                & qlive[:, None]
            )
            return attend(q_rows, do_rows, lse_rows, delta_rows, kvr_heads[0], kvr_heads[1], allow)

        def reply_skip():
            return (
                jnp.zeros((rblock, G, group_size, DH), jnp.float32),
                jnp.zeros((rblock, G, DH), jnp.float32),
                jnp.zeros((rblock, G, DH), jnp.float32),
            )

        dq_three, dk_three, dv_three = lax.cond(source <= mine, reply_block, reply_skip)
        prompt_term = jnp.stack([dk_two, dv_two]).reshape(2, pblock, kwidth)
        group_term = jnp.stack([dk_one[:, 0], dv_one[:, 0]])
        prompt_term = lax.dynamic_update_slice_in_dim(
            prompt_term, lax.dynamic_slice_in_dim(prompt_term, start, DH, 2) + group_term, start, 2
        )
        reply_term = jnp.stack([dk_three, dv_three]).reshape(2, rblock, kwidth)
        return (prompt_term, reply_term, dq_one, dq_two + dq_three)

    def fold_prompt(accp, term):
        return accp + term

    def pass_sums(accp, accr):
        return from_behind((accp, accr), "prompt", 1)

    accp_start = jnp.zeros((2, pblock, kwidth), jnp.float32)
    start_carry = (
        kv_prompt,
        kv_reply.reshape(2, rblock, kwidth),
        reply_mask[0].astype(jnp.bfloat16),
        accp_start,
        jnp.zeros((2, rblock, kwidth), jnp.float32),
        jnp.zeros((pblock, 1, heads_here, DH), jnp.float32),
        jnp.zeros((rblock, G, group_size, DH), jnp.float32),
    )

    def loop_turn(step, carry):
        kvp, kvr, maskr, accp, accr, dq_head, dq_rows = carry
        prompt_term, reply_term, dq_one, dq_two = turn_terms(step, kvp, kvr, maskr)
        accp, accr = pass_sums(fold_prompt(accp, prompt_term), accr + reply_term)
        kvp, kvr, maskr = from_behind((kvp, kvr, maskr), "prompt", 1)
        return (kvp, kvr, maskr, accp, accr, dq_head + dq_one, dq_rows + dq_two)

    kvp, kvr, maskr, accp, accr, dq_head, dq_rows = lax.fori_loop(
        0, nprompt - 1, loop_turn, start_carry
    )
    final = nprompt - 1
    prompt_term, reply_term, dq_one, dq_two = turn_terms(final, kvp, kvr, maskr)
    accp, accr = pass_sums(fold_prompt(accp, prompt_term), accr + reply_term)
    dq_head = dq_head + dq_one
    dq_rows = dq_rows + dq_two
    dkv_prompt = lax.psum(accp, "reply").astype(jnp.bfloat16)
    dq_prompt = dq_head.reshape(pblock, qwidth).astype(jnp.bfloat16)
    dq_reply = dq_rows.reshape(1, rblock, H * DH).astype(jnp.bfloat16)
    dkv_reply = accr.reshape(2, 1, rblock, kwidth).astype(jnp.bfloat16)
    return (dq_prompt, dkv_prompt, dq_reply, dkv_reply)


def solution(mesh):
    placed = (
        P("prompt", "reply"),
        P("prompt", "reply"),
        P(None, "prompt", None),
        P("reply", "prompt"),
        P("reply", "prompt"),
        P("reply", "prompt", None),
        P("reply", "prompt", None),
        P(None, "reply", "prompt", None),
        P("reply", None, "prompt"),
        P("reply", None, "prompt"),
        P("reply"),
        P("reply", "prompt"),
    )
    return jax.shard_map(
        local,
        mesh=mesh,
        in_specs=placed,
        out_specs=(
            P("prompt", "reply"),
            P(None, "prompt", None),
            P("reply", "prompt", None),
            P(None, "reply", "prompt", None),
        ),
        check_vma=False,
    )
```

profile of v0, /device:TPU:32, one launch (start us, length us, event | category | flops | bytes accessed | tf_op | source)
XLA Modules:
  0.0 810.7 jit_solution(2874332559091885960)
XLA Ops:
  10.2 606.8 %while.32 = (s32[]{:T(128)}, bf16[2,64,512]{2,1,0:T(8,128)(2,1)}, bf16[2,64,512]{2,1,0:T(8,128)(2,1)}, bf16[64]{0:T(256)(128)(2,1)}, f32[2,64,512]{2,1,0:T(8,128...) while((s32[]{:T(128)}, bf16[2,64,512]{2,1,0:T(8,128)(2,1)}, ...), condition=%wide.region_5.6_spmd.clone.clone.clone, body=%wide.region_0.5_spmd.clone.clone.clone.sunk | while | flops 344310144 | bytes 33365344 | solution.py:151
  14.9 3.5 collective-permute-start.1
  20.0 1.9 collective-permute-start
  25.7 3.9 conditional.14
  32.0 3.5 collective-permute-start.3
  35.5 6.5 conditional.15
  43.0 1.9 collective-permute-start.4
  47.4 5.4 collective-permute-done.4
  58.2 1.9 collective-permute-start.1
  61.7 1.9 collective-permute-start
  69.9 5.6 collective-permute-start.3
  78.3 6.7 collective-permute-start.4
  88.3 4.7 collective-permute-done.4
  98.4 1.9 collective-permute-start.1
  101.9 2.5 collective-permute-start
  110.6 4.4 collective-permute-start.3
  117.8 5.8 collective-permute-start.4
  126.9 6.3 collective-permute-done.4
  138.6 2.8 collective-permute-start.1
  143.0 2.1 collective-permute-start
  151.3 4.4 collective-permute-start.3
  158.5 1.9 collective-permute-start.4
  165.1 9.2 %collective-permute-done.4 = f32[2,64,512]{2,1,0:T(8,128)S(1)} collective-permute-done((f32[2,64,512]{2,1,0:T(8,128)S(1)}, f32[2,64,512]{2,1,0:T(8,128)S(1)}, u32[]{:S(2)}, u32[]{:S(2)}) %collective-permute-start.4) | collective-permute-done | bytes 262176 | tf_op jit(solution)/shard_map/while/body/eval_jaxpr/ppermute | solution.py:14
  179.7 1.9 collective-permute-start.1
  183.2 5.3 collective-permute-start
  194.7 4.4 collective-permute-start.3
  201.9 1.9 collective-permute-start.4
  207.1 7.4 collective-permute-done.4
  219.9 1.9 collective-permute-start.1
  223.4 5.3 collective-permute-start
  234.9 4.4 collective-permute-start.3
  242.0 1.9 collective-permute-start.4
  247.3 7.4 collective-permute-done.4
  260.1 1.9 collective-permute-start.1
  263.5 1.9 collective-permute-start
  271.7 5.3 collective-permute-start.3
  279.8 1.9 collective-permute-start.4
  285.6 9.2 %collective-permute-done.4 = f32[2,64,512]{2,1,0:T(8,128)S(1)} collective-permute-done((f32[2,64,512]{2,1,0:T(8,128)S(1)}, f32[2,64,512]{2,1,0:T(8,128)S(1)}, u32[]{:S(2)}, u32[]{:S(2)}) %collective-permute-start.4) | collective-permute-done | bytes 262176 | tf_op jit(solution)/shard_map/while/body/eval_jaxpr/ppermute | solution.py:14
  316.6 6.2 collective-permute-start.4
  326.1 8.9 %collective-permute-done.4 = f32[2,64,512]{2,1,0:T(8,128)S(1)} collective-permute-done((f32[2,64,512]{2,1,0:T(8,128)S(1)}, f32[2,64,512]{2,1,0:T(8,128)S(1)}, u32[]{:S(2)}, u32[]{:S(2)}) %collective-permute-start.4) | collective-permute-done | bytes 262176 | tf_op jit(solution)/shard_map/while/body/eval_jaxpr/ppermute | solution.py:14
  356.8 1.9 collective-permute-start.4
  362.0 4.0 collective-permute-done.3
  366.0 9.2 %collective-permute-done.4 = f32[2,64,512]{2,1,0:T(8,128)S(1)} collective-permute-done((f32[2,64,512]{2,1,0:T(8,128)S(1)}, f32[2,64,512]{2,1,0:T(8,128)S(1)}, u32[]{:S(2)}, u32[]{:S(2)}) %collective-permute-start.4) | collective-permute-done | bytes 262176 | tf_op jit(solution)/shard_map/while/body/eval_jaxpr/ppermute | solution.py:14
  397.0 1.9 collective-permute-start.4
  402.2 4.0 collective-permute-done.3
  406.2 9.2 %collective-permute-done.4 = f32[2,64,512]{2,1,0:T(8,128)S(1)} collective-permute-done((f32[2,64,512]{2,1,0:T(8,128)S(1)}, f32[2,64,512]{2,1,0:T(8,128)S(1)}, u32[]{:S(2)}, u32[]{:S(2)}) %collective-permute-start.4) | collective-permute-done | bytes 262176 | tf_op jit(solution)/shard_map/while/body/eval_jaxpr/ppermute | solution.py:14
  437.1 1.9 collective-permute-start.4
  442.4 4.0 collective-permute-done.3
  446.4 9.2 %collective-permute-done.4 = f32[2,64,512]{2,1,0:T(8,128)S(1)} collective-permute-done((f32[2,64,512]{2,1,0:T(8,128)S(1)}, f32[2,64,512]{2,1,0:T(8,128)S(1)}, u32[]{:S(2)}, u32[]{:S(2)}) %collective-permute-start.4) | collective-permute-done | bytes 262176 | tf_op jit(solution)/shard_map/while/body/eval_jaxpr/ppermute | solution.py:14
  477.3 1.9 collective-permute-start.4
  482.5 4.0 collective-permute-done.3
  486.5 9.2 %collective-permute-done.4 = f32[2,64,512]{2,1,0:T(8,128)S(1)} collective-permute-done((f32[2,64,512]{2,1,0:T(8,128)S(1)}, f32[2,64,512]{2,1,0:T(8,128)S(1)}, u32[]{:S(2)}, u32[]{:S(2)}) %collective-permute-start.4) | collective-permute-done | bytes 262176 | tf_op jit(solution)/shard_map/while/body/eval_jaxpr/ppermute | solution.py:14
  517.5 1.9 collective-permute-start.4
  522.7 4.0 collective-permute-done.3
  526.7 9.2 %collective-permute-done.4 = f32[2,64,512]{2,1,0:T(8,128)S(1)} collective-permute-done((f32[2,64,512]{2,1,0:T(8,128)S(1)}, f32[2,64,512]{2,1,0:T(8,128)S(1)}, u32[]{:S(2)}, u32[]{:S(2)}) %collective-permute-start.4) | collective-permute-done | bytes 262176 | tf_op jit(solution)/shard_map/while/body/eval_jaxpr/ppermute | solution.py:14
  557.7 1.9 collective-permute-start.4
  562.9 4.0 collective-permute-done.3
  566.9 9.2 %collective-permute-done.4 = f32[2,64,512]{2,1,0:T(8,128)S(1)} collective-permute-done((f32[2,64,512]{2,1,0:T(8,128)S(1)}, f32[2,64,512]{2,1,0:T(8,128)S(1)}, u32[]{:S(2)}, u32[]{:S(2)}) %collective-permute-start.4) | collective-permute-done | bytes 262176 | tf_op jit(solution)/shard_map/while/body/eval_jaxpr/ppermute | solution.py:14
  597.8 1.9 collective-permute-start.4
  603.1 4.0 collective-permute-done.3
  607.1 9.2 %collective-permute-done.4 = f32[2,64,512]{2,1,0:T(8,128)S(1)} collective-permute-done((f32[2,64,512]{2,1,0:T(8,128)S(1)}, f32[2,64,512]{2,1,0:T(8,128)S(1)}, u32[]{:S(2)}, u32[]{:S(2)}) %collective-permute-start.4) | collective-permute-done | bytes 262176 | tf_op jit(solution)/shard_map/while/body/eval_jaxpr/ppermute | solution.py:14
  630.0 1.9 collective-permute-start.6
  635.1 10.7 %collective-permute-done.6 = bf16[2,64,512]{2,1,0:T(8,128)(2,1)S(1)} collective-permute-done((bf16[2,64,512]{2,1,0:T(8,128)(2,1)S(1)}, bf16[2,64,512]{2,1,0:T(8,128)(2,1)S(1)}, u32[]{:S(2)}, u32[]{:S(2)}) %collective-permute-start.6) | collective-permute-done | bytes 131104 | tf_op jit(solution)/shard_map/ppermute | solution.py:14
  645.8 164.2 %all-reduce.1 = bf16[2,64,512]{2,1,0:T(8,128)(2,1)} all-reduce(f32[2,64,512]{2,1,0:T(8,128)} %collective-permute-done.5), channel_id=1, replica_groups=mesh['prompt'=16,'reply'=32] {'reply'}, use_global_device_ids=true, to_apply=%region_8.9 | all-reduce | flops 65536 | bytes 393216 | tf_op jit(solution)/shard_map/psum | solution.py:159
  (913 shorter events, 393.2 us)
Async XLA Ops:
  11.4 36.0 %collective-permute-start.2 = (bf16[64]{0:T(256)(128)(2,1)}, bf16[64]{0:T(256)(128)(2,1)}, u32[]{:S(2)}, u32[]{:S(2)}) collective-permute-start(bf16[64]{0:T(256)(128)(2,1)} %copy.178), channel_id=1, source_target_pairs={{480,0},{0,32},{32,64},{64,96},{96,128},{128,160},{160,192},{192,2... | collective-permute-start | bytes 392 | tf_op jit(solution)/shard_map/while/body/eval_jaxpr/ppermute | solution.py:14
  14.9 32.5 %collective-permute-start.1 = (bf16[2,64,512]{2,1,0:T(8,128)(2,1)}, bf16[2,64,512]{2,1,0:T(8,128)(2,1)}, u32[]{:S(2)}, u32[]{:S(2)}) collective-permute-start(bf16[2,64,512]{2,1,0:T(8,128)(2,1)} %copy.177), channel_id=1, source_target_pairs={{480,0},{0,32},{32,64},{64,96},{96,128},{128,160},{160,192},{192,2... | collective-permute-start | bytes 393224 | tf_op jit(solution)/shard_map/while/body/eval_jaxpr/ppermute | solution.py:14
  20.0 27.4 %collective-permute-start = (bf16[2,64,512]{2,1,0:T(8,128)(2,1)}, bf16[2,64,512]{2,1,0:T(8,128)(2,1)}, u32[]{:S(2)}, u32[]{:S(2)}) collective-permute-start(bf16[2,64,512]{2,1,0:T(8,128)(2,1)} %copy.176), channel_id=1, source_target_pairs={{480,0},{0,32},{32,64},{64,96},{96,128},{128,160},{160,192},{192,2... | collective-permute-start | bytes 393224 | tf_op jit(solution)/shard_map/while/body/eval_jaxpr/ppermute | solution.py:14
  32.0 15.4 %collective-permute-start.3 = (f32[2,64,512]{2,1,0:T(8,128)}, f32[2,64,512]{2,1,0:T(8,128)}, u32[]{:S(2)}, u32[]{:S(2)}) collective-permute-start(f32[2,64,512]{2,1,0:T(8,128)} %add.323), channel_id=1, source_target_pairs={{480,0},{0,32},{32,64},{64,96},{96,128},{128,160},{160,192},{192,2... | collective-permute-start | bytes 786440 | tf_op jit(solution)/shard_map/while/body/eval_jaxpr/ppermute | solution.py:14
  54.7 33.6 %collective-permute-start.2 = (bf16[64]{0:T(256)(128)(2,1)}, bf16[64]{0:T(256)(128)(2,1)}, u32[]{:S(2)}, u32[]{:S(2)}) collective-permute-start(bf16[64]{0:T(256)(128)(2,1)} %copy.178), channel_id=1, source_target_pairs={{480,0},{0,32},{32,64},{64,96},{96,128},{128,160},{160,192},{192,2... | collective-permute-start | bytes 392 | tf_op jit(solution)/shard_map/while/body/eval_jaxpr/ppermute | solution.py:14
  58.2 30.1 %collective-permute-start.1 = (bf16[2,64,512]{2,1,0:T(8,128)(2,1)}, bf16[2,64,512]{2,1,0:T(8,128)(2,1)}, u32[]{:S(2)}, u32[]{:S(2)}) collective-permute-start(bf16[2,64,512]{2,1,0:T(8,128)(2,1)} %copy.177), channel_id=1, source_target_pairs={{480,0},{0,32},{32,64},{64,96},{96,128},{128,160},{160,192},{192,2... | collective-permute-start | bytes 393224 | tf_op jit(solution)/shard_map/while/body/eval_jaxpr/ppermute | solution.py:14
  61.7 26.6 %collective-permute-start = (bf16[2,64,512]{2,1,0:T(8,128)(2,1)}, bf16[2,64,512]{2,1,0:T(8,128)(2,1)}, u32[]{:S(2)}, u32[]{:S(2)}) collective-permute-start(bf16[2,64,512]{2,1,0:T(8,128)(2,1)} %copy.176), channel_id=1, source_target_pairs={{480,0},{0,32},{32,64},{64,96},{96,128},{128,160},{160,192},{192,2... | collective-permute-start | bytes 393224 | tf_op jit(solution)/shard_map/while/body/eval_jaxpr/ppermute | solution.py:14
  69.9 18.5 %collective-permute-start.3 = (f32[2,64,512]{2,1,0:T(8,128)}, f32[2,64,512]{2,1,0:T(8,128)}, u32[]{:S(2)}, u32[]{:S(2)}) collective-permute-start(f32[2,64,512]{2,1,0:T(8,128)} %add.323), channel_id=1, source_target_pairs={{480,0},{0,32},{32,64},{64,96},{96,128},{128,160},{160,192},{192,2... | collective-permute-start | bytes 786440 | tf_op jit(solution)/shard_map/while/body/eval_jaxpr/ppermute | solution.py:14
  78.3 14.7 %collective-permute-start.4 = (f32[2,64,512]{2,1,0:T(8,128)S(1)}, f32[2,64,512]{2,1,0:T(8,128)S(1)}, u32[]{:S(2)}, u32[]{:S(2)}) collective-permute-start(f32[2,64,512]{2,1,0:T(8,128)S(1)} %maximum_add_fusion.5), channel_id=1, source_target_pairs={{480,0},{0,32},{32,64},{64,96},{96,128},{128,160},{160,192},{192,2... | collective-permute-start | bytes 786440 | tf_op jit(solution)/shard_map/while/body/eval_jaxpr/ppermute | solution.py:14
  94.9 32.0 %collective-permute-start.2 = (bf16[64]{0:T(256)(128)(2,1)}, bf16[64]{0:T(256)(128)(2,1)}, u32[]{:S(2)}, u32[]{:S(2)}) collective-permute-start(bf16[64]{0:T(256)(128)(2,1)} %copy.178), channel_id=1, source_target_pairs={{480,0},{0,32},{32,64},{64,96},{96,128},{128,160},{160,192},{192,2... | collective-permute-start | bytes 392 | tf_op jit(solution)/shard_map/while/body/eval_jaxpr/ppermute | solution.py:14
  98.4 28.5 %collective-permute-start.1 = (bf16[2,64,512]{2,1,0:T(8,128)(2,1)}, bf16[2,64,512]{2,1,0:T(8,128)(2,1)}, u32[]{:S(2)}, u32[]{:S(2)}) collective-permute-start(bf16[2,64,512]{2,1,0:T(8,128)(2,1)} %copy.177), channel_id=1, source_target_pairs={{480,0},{0,32},{32,64},{64,96},{96,128},{128,160},{160,192},{192,2... | collective-permute-start | bytes 393224 | tf_op jit(solution)/shard_map/while/body/eval_jaxpr/ppermute | solution.py:14
  101.9 25.0 %collective-permute-start = (bf16[2,64,512]{2,1,0:T(8,128)(2,1)}, bf16[2,64,512]{2,1,0:T(8,128)(2,1)}, u32[]{:S(2)}, u32[]{:S(2)}) collective-permute-start(bf16[2,64,512]{2,1,0:T(8,128)(2,1)} %copy.176), channel_id=1, source_target_pairs={{480,0},{0,32},{32,64},{64,96},{96,128},{128,160},{160,192},{192,2... | collective-permute-start | bytes 393224 | tf_op jit(solution)/shard_map/while/body/eval_jaxpr/ppermute | solution.py:14
  110.6 16.3 %collective-permute-start.3 = (f32[2,64,512]{2,1,0:T(8,128)}, f32[2,64,512]{2,1,0:T(8,128)}, u32[]{:S(2)}, u32[]{:S(2)}) collective-permute-start(f32[2,64,512]{2,1,0:T(8,128)} %add.323), channel_id=1, source_target_pairs={{480,0},{0,32},{32,64},{64,96},{96,128},{128,160},{160,192},{192,2... | collective-permute-start | bytes 786440 | tf_op jit(solution)/shard_map/while/body/eval_jaxpr/ppermute | solution.py:14
  117.8 15.4 %collective-permute-start.4 = (f32[2,64,512]{2,1,0:T(8,128)S(1)}, f32[2,64,512]{2,1,0:T(8,128)S(1)}, u32[]{:S(2)}, u32[]{:S(2)}) collective-permute-start(f32[2,64,512]{2,1,0:T(8,128)S(1)} %maximum_add_fusion.5), channel_id=1, source_target_pairs={{480,0},{0,32},{32,64},{64,96},{96,128},{128,160},{160,192},{192,2... | collective-permute-start | bytes 786440 | tf_op jit(solution)/shard_map/while/body/eval_jaxpr/ppermute | solution.py:14
  135.1 28.6 %collective-permute-start.2 = (bf16[64]{0:T(256)(128)(2,1)}, bf16[64]{0:T(256)(128)(2,1)}, u32[]{:S(2)}, u32[]{:S(2)}) collective-permute-start(bf16[64]{0:T(256)(128)(2,1)} %copy.178), channel_id=1, source_target_pairs={{480,0},{0,32},{32,64},{64,96},{96,128},{128,160},{160,192},{192,2... | collective-permute-start | bytes 392 | tf_op jit(solution)/shard_map/while/body/eval_jaxpr/ppermute | solution.py:14
  138.6 25.2 %collective-permute-start.1 = (bf16[2,64,512]{2,1,0:T(8,128)(2,1)}, bf16[2,64,512]{2,1,0:T(8,128)(2,1)}, u32[]{:S(2)}, u32[]{:S(2)}) collective-permute-start(bf16[2,64,512]{2,1,0:T(8,128)(2,1)} %copy.177), channel_id=1, source_target_pairs={{480,0},{0,32},{32,64},{64,96},{96,128},{128,160},{160,192},{192,2... | collective-permute-start | bytes 393224 | tf_op jit(solution)/shard_map/while/body/eval_jaxpr/ppermute | solution.py:14
  143.0 20.7 %collective-permute-start = (bf16[2,64,512]{2,1,0:T(8,128)(2,1)}, bf16[2,64,512]{2,1,0:T(8,128)(2,1)}, u32[]{:S(2)}, u32[]{:S(2)}) collective-permute-start(bf16[2,64,512]{2,1,0:T(8,128)(2,1)} %copy.176), channel_id=1, source_target_pairs={{480,0},{0,32},{32,64},{64,96},{96,128},{128,160},{160,192},{192,2... | collective-permute-start | bytes 393224 | tf_op jit(solution)/shard_map/while/body/eval_jaxpr/ppermute | solution.py:14
  158.5 15.8 %collective-permute-start.4 = (f32[2,64,512]{2,1,0:T(8,128)S(1)}, f32[2,64,512]{2,1,0:T(8,128)S(1)}, u32[]{:S(2)}, u32[]{:S(2)}) collective-permute-start(f32[2,64,512]{2,1,0:T(8,128)S(1)} %maximum_add_fusion.5), channel_id=1, source_target_pairs={{480,0},{0,32},{32,64},{64,96},{96,128},{128,160},{160,192},{192,2... | collective-permute-start | bytes 786440 | tf_op jit(solution)/shard_map/while/body/eval_jaxpr/ppermute | solution.py:14
  176.2 30.9 %collective-permute-start.2 = (bf16[64]{0:T(256)(128)(2,1)}, bf16[64]{0:T(256)(128)(2,1)}, u32[]{:S(2)}, u32[]{:S(2)}) collective-permute-start(bf16[64]{0:T(256)(128)(2,1)} %copy.178), channel_id=1, source_target_pairs={{480,0},{0,32},{32,64},{64,96},{96,128},{128,160},{160,192},{192,2... | collective-permute-start | bytes 392 | tf_op jit(solution)/shard_map/while/body/eval_jaxpr/ppermute | solution.py:14
  179.7 27.4 %collective-permute-start.1 = (bf16[2,64,512]{2,1,0:T(8,128)(2,1)}, bf16[2,64,512]{2,1,0:T(8,128)(2,1)}, u32[]{:S(2)}, u32[]{:S(2)}) collective-permute-start(bf16[2,64,512]{2,1,0:T(8,128)(2,1)} %copy.177), channel_id=1, source_target_pairs={{480,0},{0,32},{32,64},{64,96},{96,128},{128,160},{160,192},{192,2... | collective-permute-start | bytes 393224 | tf_op jit(solution)/shard_map/while/body/eval_jaxpr/ppermute | solution.py:14
  183.2 23.9 %collective-permute-start = (bf16[2,64,512]{2,1,0:T(8,128)(2,1)}, bf16[2,64,512]{2,1,0:T(8,128)(2,1)}, u32[]{:S(2)}, u32[]{:S(2)}) collective-permute-start(bf16[2,64,512]{2,1,0:T(8,128)(2,1)} %copy.176), channel_id=1, source_target_pairs={{480,0},{0,32},{32,64},{64,96},{96,128},{128,160},{160,192},{192,2... | collective-permute-start | bytes 393224 | tf_op jit(solution)/shard_map/while/body/eval_jaxpr/ppermute | solution.py:14
  216.4 30.9 %collective-permute-start.2 = (bf16[64]{0:T(256)(128)(2,1)}, bf16[64]{0:T(256)(128)(2,1)}, u32[]{:S(2)}, u32[]{:S(2)}) collective-permute-start(bf16[64]{0:T(256)(128)(2,1)} %copy.178), channel_id=1, source_target_pairs={{480,0},{0,32},{32,64},{64,96},{96,128},{128,160},{160,192},{192,2... | collective-permute-start | bytes 392 | tf_op jit(solution)/shard_map/while/body/eval_jaxpr/ppermute | solution.py:14
  219.9 27.4 %collective-permute-start.1 = (bf16[2,64,512]{2,1,0:T(8,128)(2,1)}, bf16[2,64,512]{2,1,0:T(8,128)(2,1)}, u32[]{:S(2)}, u32[]{:S(2)}) collective-permute-start(bf16[2,64,512]{2,1,0:T(8,128)(2,1)} %copy.177), channel_id=1, source_target_pairs={{480,0},{0,32},{32,64},{64,96},{96,128},{128,160},{160,192},{192,2... | collective-permute-start | bytes 393224 | tf_op jit(solution)/shard_map/while/body/eval_jaxpr/ppermute | solution.py:14
  223.4 23.9 %collective-permute-start = (bf16[2,64,512]{2,1,0:T(8,128)(2,1)}, bf16[2,64,512]{2,1,0:T(8,128)(2,1)}, u32[]{:S(2)}, u32[]{:S(2)}) collective-permute-start(bf16[2,64,512]{2,1,0:T(8,128)(2,1)} %copy.176), channel_id=1, source_target_pairs={{480,0},{0,32},{32,64},{64,96},{96,128},{128,160},{160,192},{192,2... | collective-permute-start | bytes 393224 | tf_op jit(solution)/shard_map/while/body/eval_jaxpr/ppermute | solution.py:14
  256.6 28.4 %collective-permute-start.2 = (bf16[64]{0:T(256)(128)(2,1)}, bf16[64]{0:T(256)(128)(2,1)}, u32[]{:S(2)}, u32[]{:S(2)}) collective-permute-start(bf16[64]{0:T(256)(128)(2,1)} %copy.178), channel_id=1, source_target_pairs={{480,0},{0,32},{32,64},{64,96},{96,128},{128,160},{160,192},{192,2... | collective-permute-start | bytes 392 | tf_op jit(solution)/shard_map/while/body/eval_jaxpr/ppermute | solution.py:14
  260.1 25.0 %collective-permute-start.1 = (bf16[2,64,512]{2,1,0:T(8,128)(2,1)}, bf16[2,64,512]{2,1,0:T(8,128)(2,1)}, u32[]{:S(2)}, u32[]{:S(2)}) collective-permute-start(bf16[2,64,512]{2,1,0:T(8,128)(2,1)} %copy.177), channel_id=1, source_target_pairs={{480,0},{0,32},{32,64},{64,96},{96,128},{128,160},{160,192},{192,2... | collective-permute-start | bytes 393224 | tf_op jit(solution)/shard_map/while/body/eval_jaxpr/ppermute | solution.py:14
  263.5 21.5 %collective-permute-start = (bf16[2,64,512]{2,1,0:T(8,128)(2,1)}, bf16[2,64,512]{2,1,0:T(8,128)(2,1)}, u32[]{:S(2)}, u32[]{:S(2)}) collective-permute-start(bf16[2,64,512]{2,1,0:T(8,128)(2,1)} %copy.176), channel_id=1, source_target_pairs={{480,0},{0,32},{32,64},{64,96},{96,128},{128,160},{160,192},{192,2... | collective-permute-start | bytes 393224 | tf_op jit(solution)/shard_map/while/body/eval_jaxpr/ppermute | solution.py:14
  271.7 14.0 %collective-permute-start.3 = (f32[2,64,512]{2,1,0:T(8,128)}, f32[2,64,512]{2,1,0:T(8,128)}, u32[]{:S(2)}, u32[]{:S(2)}) collective-permute-start(f32[2,64,512]{2,1,0:T(8,128)} %add.323), channel_id=1, source_target_pairs={{480,0},{0,32},{32,64},{64,96},{96,128},{128,160},{160,192},{192,2... | collective-permute-start | bytes 786440 | tf_op jit(solution)/shard_map/while/body/eval_jaxpr/ppermute | solution.py:14
  279.8 15.1 %collective-permute-start.4 = (f32[2,64,512]{2,1,0:T(8,128)S(1)}, f32[2,64,512]{2,1,0:T(8,128)S(1)}, u32[]{:S(2)}, u32[]{:S(2)}) collective-permute-start(f32[2,64,512]{2,1,0:T(8,128)S(1)} %maximum_add_fusion.5), channel_id=1, source_target_pairs={{480,0},{0,32},{32,64},{64,96},{96,128},{128,160},{160,192},{192,2... | collective-permute-start | bytes 786440 | tf_op jit(solution)/shard_map/while/body/eval_jaxpr/ppermute | solution.py:14
  296.7 29.4 %collective-permute-start.2 = (bf16[64]{0:T(256)(128)(2,1)}, bf16[64]{0:T(256)(128)(2,1)}, u32[]{:S(2)}, u32[]{:S(2)}) collective-permute-start(bf16[64]{0:T(256)(128)(2,1)} %copy.178), channel_id=1, source_target_pairs={{480,0},{0,32},{32,64},{64,96},{96,128},{128,160},{160,192},{192,2... | collective-permute-start | bytes 392 | tf_op jit(solution)/shard_map/while/body/eval_jaxpr/ppermute | solution.py:14
  300.2 25.9 %collective-permute-start.1 = (bf16[2,64,512]{2,1,0:T(8,128)(2,1)}, bf16[2,64,512]{2,1,0:T(8,128)(2,1)}, u32[]{:S(2)}, u32[]{:S(2)}) collective-permute-start(bf16[2,64,512]{2,1,0:T(8,128)(2,1)} %copy.177), channel_id=1, source_target_pairs={{480,0},{0,32},{32,64},{64,96},{96,128},{128,160},{160,192},{192,2... | collective-permute-start | bytes 393224 | tf_op jit(solution)/shard_map/while/body/eval_jaxpr/ppermute | solution.py:14
  303.7 22.4 %collective-permute-start = (bf16[2,64,512]{2,1,0:T(8,128)(2,1)}, bf16[2,64,512]{2,1,0:T(8,128)(2,1)}, u32[]{:S(2)}, u32[]{:S(2)}) collective-permute-start(bf16[2,64,512]{2,1,0:T(8,128)(2,1)} %copy.176), channel_id=1, source_target_pairs={{480,0},{0,32},{32,64},{64,96},{96,128},{128,160},{160,192},{192,2... | collective-permute-start | bytes 393224 | tf_op jit(solution)/shard_map/while/body/eval_jaxpr/ppermute | solution.py:14
  311.9 14.3 %collective-permute-start.3 = (f32[2,64,512]{2,1,0:T(8,128)}, f32[2,64,512]{2,1,0:T(8,128)}, u32[]{:S(2)}, u32[]{:S(2)}) collective-permute-start(f32[2,64,512]{2,1,0:T(8,128)} %add.323), channel_id=1, source_target_pairs={{480,0},{0,32},{32,64},{64,96},{96,128},{128,160},{160,192},{192,2... | collective-permute-start | bytes 786440 | tf_op jit(solution)/shard_map/while/body/eval_jaxpr/ppermute | solution.py:14
  316.6 18.4 %collective-permute-start.4 = (f32[2,64,512]{2,1,0:T(8,128)S(1)}, f32[2,64,512]{2,1,0:T(8,128)S(1)}, u32[]{:S(2)}, u32[]{:S(2)}) collective-permute-start(f32[2,64,512]{2,1,0:T(8,128)S(1)} %maximum_add_fusion.5), channel_id=1, source_target_pairs={{480,0},{0,32},{32,64},{64,96},{96,128},{128,160},{160,192},{192,2... | collective-permute-start | bytes 786440 | tf_op jit(solution)/shard_map/while/body/eval_jaxpr/ppermute | solution.py:14
  336.9 25.1 %collective-permute-start.2 = (bf16[64]{0:T(256)(128)(2,1)}, bf16[64]{0:T(256)(128)(2,1)}, u32[]{:S(2)}, u32[]{:S(2)}) collective-permute-start(bf16[64]{0:T(256)(128)(2,1)} %copy.178), channel_id=1, source_target_pairs={{480,0},{0,32},{32,64},{64,96},{96,128},{128,160},{160,192},{192,2... | collective-permute-start | bytes 392 | tf_op jit(solution)/shard_map/while/body/eval_jaxpr/ppermute | solution.py:14
  340.4 21.6 %collective-permute-start.1 = (bf16[2,64,512]{2,1,0:T(8,128)(2,1)}, bf16[2,64,512]{2,1,0:T(8,128)(2,1)}, u32[]{:S(2)}, u32[]{:S(2)}) collective-permute-start(bf16[2,64,512]{2,1,0:T(8,128)(2,1)} %copy.177), channel_id=1, source_target_pairs={{480,0},{0,32},{32,64},{64,96},{96,128},{128,160},{160,192},{192,2... | collective-permute-start | bytes 393224 | tf_op jit(solution)/shard_map/while/body/eval_jaxpr/ppermute | solution.py:14
  343.9 18.1 %collective-permute-start = (bf16[2,64,512]{2,1,0:T(8,128)(2,1)}, bf16[2,64,512]{2,1,0:T(8,128)(2,1)}, u32[]{:S(2)}, u32[]{:S(2)}) collective-permute-start(bf16[2,64,512]{2,1,0:T(8,128)(2,1)} %copy.176), channel_id=1, source_target_pairs={{480,0},{0,32},{32,64},{64,96},{96,128},{128,160},{160,192},{192,2... | collective-permute-start | bytes 393224 | tf_op jit(solution)/shard_map/while/body/eval_jaxpr/ppermute | solution.py:14
  356.8 18.4 %collective-permute-start.4 = (f32[2,64,512]{2,1,0:T(8,128)S(1)}, f32[2,64,512]{2,1,0:T(8,128)S(1)}, u32[]{:S(2)}, u32[]{:S(2)}) collective-permute-start(f32[2,64,512]{2,1,0:T(8,128)S(1)} %maximum_add_fusion.5), channel_id=1, source_target_pairs={{480,0},{0,32},{32,64},{64,96},{96,128},{128,160},{160,192},{192,2... | collective-permute-start | bytes 786440 | tf_op jit(solution)/shard_map/while/body/eval_jaxpr/ppermute | solution.py:14
  377.1 25.1 %collective-permute-start.2 = (bf16[64]{0:T(256)(128)(2,1)}, bf16[64]{0:T(256)(128)(2,1)}, u32[]{:S(2)}, u32[]{:S(2)}) collective-permute-start(bf16[64]{0:T(256)(128)(2,1)} %copy.178), channel_id=1, source_target_pairs={{480,0},{0,32},{32,64},{64,96},{96,128},{128,160},{160,192},{192,2... | collective-permute-start | bytes 392 | tf_op jit(solution)/shard_map/while/body/eval_jaxpr/ppermute | solution.py:14
  380.6 21.6 %collective-permute-start.1 = (bf16[2,64,512]{2,1,0:T(8,128)(2,1)}, bf16[2,64,512]{2,1,0:T(8,128)(2,1)}, u32[]{:S(2)}, u32[]{:S(2)}) collective-permute-start(bf16[2,64,512]{2,1,0:T(8,128)(2,1)} %copy.177), channel_id=1, source_target_pairs={{480,0},{0,32},{32,64},{64,96},{96,128},{128,160},{160,192},{192,2... | collective-permute-start | bytes 393224 | tf_op jit(solution)/shard_map/while/body/eval_jaxpr/ppermute | solution.py:14
  384.1 18.1 %collective-permute-start = (bf16[2,64,512]{2,1,0:T(8,128)(2,1)}, bf16[2,64,512]{2,1,0:T(8,128)(2,1)}, u32[]{:S(2)}, u32[]{:S(2)}) collective-permute-start(bf16[2,64,512]{2,1,0:T(8,128)(2,1)} %copy.176), channel_id=1, source_target_pairs={{480,0},{0,32},{32,64},{64,96},{96,128},{128,160},{160,192},{192,2... | collective-permute-start | bytes 393224 | tf_op jit(solution)/shard_map/while/body/eval_jaxpr/ppermute | solution.py:14
  397.0 18.4 %collective-permute-start.4 = (f32[2,64,512]{2,1,0:T(8,128)S(1)}, f32[2,64,512]{2,1,0:T(8,128)S(1)}, u32[]{:S(2)}, u32[]{:S(2)}) collective-permute-start(f32[2,64,512]{2,1,0:T(8,128)S(1)} %maximum_add_fusion.5), channel_id=1, source_target_pairs={{480,0},{0,32},{32,64},{64,96},{96,128},{128,160},{160,192},{192,2... | collective-permute-start | bytes 786440 | tf_op jit(solution)/shard_map/while/body/eval_jaxpr/ppermute | solution.py:14
  417.3 25.1 %collective-permute-start.2 = (bf16[64]{0:T(256)(128)(2,1)}, bf16[64]{0:T(256)(128)(2,1)}, u32[]{:S(2)}, u32[]{:S(2)}) collective-permute-start(bf16[64]{0:T(256)(128)(2,1)} %copy.178), channel_id=1, source_target_pairs={{480,0},{0,32},{32,64},{64,96},{96,128},{128,160},{160,192},{192,2... | collective-permute-start | bytes 392 | tf_op jit(solution)/shard_map/while/body/eval_jaxpr/ppermute | solution.py:14
  420.8 21.6 %collective-permute-start.1 = (bf16[2,64,512]{2,1,0:T(8,128)(2,1)}, bf16[2,64,512]{2,1,0:T(8,128)(2,1)}, u32[]{:S(2)}, u32[]{:S(2)}) collective-permute-start(bf16[2,64,512]{2,1,0:T(8,128)(2,1)} %copy.177), channel_id=1, source_target_pairs={{480,0},{0,32},{32,64},{64,96},{96,128},{128,160},{160,192},{192,2... | collective-permute-start | bytes 393224 | tf_op jit(solution)/shard_map/while/body/eval_jaxpr/ppermute | solution.py:14
  424.2 18.1 %collective-permute-start = (bf16[2,64,512]{2,1,0:T(8,128)(2,1)}, bf16[2,64,512]{2,1,0:T(8,128)(2,1)}, u32[]{:S(2)}, u32[]{:S(2)}) collective-permute-start(bf16[2,64,512]{2,1,0:T(8,128)(2,1)} %copy.176), channel_id=1, source_target_pairs={{480,0},{0,32},{32,64},{64,96},{96,128},{128,160},{160,192},{192,2... | collective-permute-start | bytes 393224 | tf_op jit(solution)/shard_map/while/body/eval_jaxpr/ppermute | solution.py:14
  437.1 18.4 %collective-permute-start.4 = (f32[2,64,512]{2,1,0:T(8,128)S(1)}, f32[2,64,512]{2,1,0:T(8,128)S(1)}, u32[]{:S(2)}, u32[]{:S(2)}) collective-permute-start(f32[2,64,512]{2,1,0:T(8,128)S(1)} %maximum_add_fusion.5), channel_id=1, source_target_pairs={{480,0},{0,32},{32,64},{64,96},{96,128},{128,160},{160,192},{192,2... | collective-permute-start | bytes 786440 | tf_op jit(solution)/shard_map/while/body/eval_jaxpr/ppermute | solution.py:14
  457.5 25.1 %collective-permute-start.2 = (bf16[64]{0:T(256)(128)(2,1)}, bf16[64]{0:T(256)(128)(2,1)}, u32[]{:S(2)}, u32[]{:S(2)}) collective-permute-start(bf16[64]{0:T(256)(128)(2,1)} %copy.178), channel_id=1, source_target_pairs={{480,0},{0,32},{32,64},{64,96},{96,128},{128,160},{160,192},{192,2... | collective-permute-start | bytes 392 | tf_op jit(solution)/shard_map/while/body/eval_jaxpr/ppermute | solution.py:14
  460.9 21.6 %collective-permute-start.1 = (bf16[2,64,512]{2,1,0:T(8,128)(2,1)}, bf16[2,64,512]{2,1,0:T(8,128)(2,1)}, u32[]{:S(2)}, u32[]{:S(2)}) collective-permute-start(bf16[2,64,512]{2,1,0:T(8,128)(2,1)} %copy.177), channel_id=1, source_target_pairs={{480,0},{0,32},{32,64},{64,96},{96,128},{128,160},{160,192},{192,2... | collective-permute-start | bytes 393224 | tf_op jit(solution)/shard_map/while/body/eval_jaxpr/ppermute | solution.py:14
  464.4 18.1 %collective-permute-start = (bf16[2,64,512]{2,1,0:T(8,128)(2,1)}, bf16[2,64,512]{2,1,0:T(8,128)(2,1)}, u32[]{:S(2)}, u32[]{:S(2)}) collective-permute-start(bf16[2,64,512]{2,1,0:T(8,128)(2,1)} %copy.176), channel_id=1, source_target_pairs={{480,0},{0,32},{32,64},{64,96},{96,128},{128,160},{160,192},{192,2... | collective-permute-start | bytes 393224 | tf_op jit(solution)/shard_map/while/body/eval_jaxpr/ppermute | solution.py:14
  477.3 18.4 %collective-permute-start.4 = (f32[2,64,512]{2,1,0:T(8,128)S(1)}, f32[2,64,512]{2,1,0:T(8,128)S(1)}, u32[]{:S(2)}, u32[]{:S(2)}) collective-permute-start(f32[2,64,512]{2,1,0:T(8,128)S(1)} %maximum_add_fusion.5), channel_id=1, source_target_pairs={{480,0},{0,32},{32,64},{64,96},{96,128},{128,160},{160,192},{192,2... | collective-permute-start | bytes 786440 | tf_op jit(solution)/shard_map/while/body/eval_jaxpr/ppermute | solution.py:14
  497.6 25.1 %collective-permute-start.2 = (bf16[64]{0:T(256)(128)(2,1)}, bf16[64]{0:T(256)(128)(2,1)}, u32[]{:S(2)}, u32[]{:S(2)}) collective-permute-start(bf16[64]{0:T(256)(128)(2,1)} %copy.178), channel_id=1, source_target_pairs={{480,0},{0,32},{32,64},{64,96},{96,128},{128,160},{160,192},{192,2... | collective-permute-start | bytes 392 | tf_op jit(solution)/shard_map/while/body/eval_jaxpr/ppermute | solution.py:14
  501.1 21.6 %collective-permute-start.1 = (bf16[2,64,512]{2,1,0:T(8,128)(2,1)}, bf16[2,64,512]{2,1,0:T(8,128)(2,1)}, u32[]{:S(2)}, u32[]{:S(2)}) collective-permute-start(bf16[2,64,512]{2,1,0:T(8,128)(2,1)} %copy.177), channel_id=1, source_target_pairs={{480,0},{0,32},{32,64},{64,96},{96,128},{128,160},{160,192},{192,2... | collective-permute-start | bytes 393224 | tf_op jit(solution)/shard_map/while/body/eval_jaxpr/ppermute | solution.py:14
  504.6 18.1 %collective-permute-start = (bf16[2,64,512]{2,1,0:T(8,128)(2,1)}, bf16[2,64,512]{2,1,0:T(8,128)(2,1)}, u32[]{:S(2)}, u32[]{:S(2)}) collective-permute-start(bf16[2,64,512]{2,1,0:T(8,128)(2,1)} %copy.176), channel_id=1, source_target_pairs={{480,0},{0,32},{32,64},{64,96},{96,128},{128,160},{160,192},{192,2... | collective-permute-start | bytes 393224 | tf_op jit(solution)/shard_map/while/body/eval_jaxpr/ppermute | solution.py:14
  517.5 18.4 %collective-permute-start.4 = (f32[2,64,512]{2,1,0:T(8,128)S(1)}, f32[2,64,512]{2,1,0:T(8,128)S(1)}, u32[]{:S(2)}, u32[]{:S(2)}) collective-permute-start(f32[2,64,512]{2,1,0:T(8,128)S(1)} %maximum_add_fusion.5), channel_id=1, source_target_pairs={{480,0},{0,32},{32,64},{64,96},{96,128},{128,160},{160,192},{192,2... | collective-permute-start | bytes 786440 | tf_op jit(solution)/shard_map/while/body/eval_jaxpr/ppermute | solution.py:14
  537.8 25.1 %collective-permute-start.2 = (bf16[64]{0:T(256)(128)(2,1)}, bf16[64]{0:T(256)(128)(2,1)}, u32[]{:S(2)}, u32[]{:S(2)}) collective-permute-start(bf16[64]{0:T(256)(128)(2,1)} %copy.178), channel_id=1, source_target_pairs={{480,0},{0,32},{32,64},{64,96},{96,128},{128,160},{160,192},{192,2... | collective-permute-start | bytes 392 | tf_op jit(solution)/shard_map/while/body/eval_jaxpr/ppermute | solution.py:14
  541.3 21.6 %collective-permute-start.1 = (bf16[2,64,512]{2,1,0:T(8,128)(2,1)}, bf16[2,64,512]{2,1,0:T(8,128)(2,1)}, u32[]{:S(2)}, u32[]{:S(2)}) collective-permute-start(bf16[2,64,512]{2,1,0:T(8,128)(2,1)} %copy.177), channel_id=1, source_target_pairs={{480,0},{0,32},{32,64},{64,96},{96,128},{128,160},{160,192},{192,2... | collective-permute-start | bytes 393224 | tf_op jit(solution)/shard_map/while/body/eval_jaxpr/ppermute | solution.py:14
  544.8 18.1 %collective-permute-start = (bf16[2,64,512]{2,1,0:T(8,128)(2,1)}, bf16[2,64,512]{2,1,0:T(8,128)(2,1)}, u32[]{:S(2)}, u32[]{:S(2)}) collective-permute-start(bf16[2,64,512]{2,1,0:T(8,128)(2,1)} %copy.176), channel_id=1, source_target_pairs={{480,0},{0,32},{32,64},{64,96},{96,128},{128,160},{160,192},{192,2... | collective-permute-start | bytes 393224 | tf_op jit(solution)/shard_map/while/body/eval_jaxpr/ppermute | solution.py:14
  557.7 18.4 %collective-permute-start.4 = (f32[2,64,512]{2,1,0:T(8,128)S(1)}, f32[2,64,512]{2,1,0:T(8,128)S(1)}, u32[]{:S(2)}, u32[]{:S(2)}) collective-permute-start(f32[2,64,512]{2,1,0:T(8,128)S(1)} %maximum_add_fusion.5), channel_id=1, source_target_pairs={{480,0},{0,32},{32,64},{64,96},{96,128},{128,160},{160,192},{192,2... | collective-permute-start | bytes 786440 | tf_op jit(solution)/shard_map/while/body/eval_jaxpr/ppermute | solution.py:14
  578.0 25.1 %collective-permute-start.2 = (bf16[64]{0:T(256)(128)(2,1)}, bf16[64]{0:T(256)(128)(2,1)}, u32[]{:S(2)}, u32[]{:S(2)}) collective-permute-start(bf16[64]{0:T(256)(128)(2,1)} %copy.178), channel_id=1, source_target_pairs={{480,0},{0,32},{32,64},{64,96},{96,128},{128,160},{160,192},{192,2... | collective-permute-start | bytes 392 | tf_op jit(solution)/shard_map/while/body/eval_jaxpr/ppermute | solution.py:14
  581.5 21.6 %collective-permute-start.1 = (bf16[2,64,512]{2,1,0:T(8,128)(2,1)}, bf16[2,64,512]{2,1,0:T(8,128)(2,1)}, u32[]{:S(2)}, u32[]{:S(2)}) collective-permute-start(bf16[2,64,512]{2,1,0:T(8,128)(2,1)} %copy.177), channel_id=1, source_target_pairs={{480,0},{0,32},{32,64},{64,96},{96,128},{128,160},{160,192},{192,2... | collective-permute-start | bytes 393224 | tf_op jit(solution)/shard_map/while/body/eval_jaxpr/ppermute | solution.py:14
  585.0 18.1 %collective-permute-start = (bf16[2,64,512]{2,1,0:T(8,128)(2,1)}, bf16[2,64,512]{2,1,0:T(8,128)(2,1)}, u32[]{:S(2)}, u32[]{:S(2)}) collective-permute-start(bf16[2,64,512]{2,1,0:T(8,128)(2,1)} %copy.176), channel_id=1, source_target_pairs={{480,0},{0,32},{32,64},{64,96},{96,128},{128,160},{160,192},{192,2... | collective-permute-start | bytes 393224 | tf_op jit(solution)/shard_map/while/body/eval_jaxpr/ppermute | solution.py:14
  597.8 18.4 %collective-permute-start.4 = (f32[2,64,512]{2,1,0:T(8,128)S(1)}, f32[2,64,512]{2,1,0:T(8,128)S(1)}, u32[]{:S(2)}, u32[]{:S(2)}) collective-permute-start(f32[2,64,512]{2,1,0:T(8,128)S(1)} %maximum_add_fusion.5), channel_id=1, source_target_pairs={{480,0},{0,32},{32,64},{64,96},{96,128},{128,160},{160,192},{192,2... | collective-permute-start | bytes 786440 | tf_op jit(solution)/shard_map/while/body/eval_jaxpr/ppermute | solution.py:14
  624.9 21.0 %collective-permute-start.5 = (f32[2,64,512]{2,1,0:T(8,128)}, f32[2,64,512]{2,1,0:T(8,128)}, u32[]{:S(2)}, u32[]{:S(2)}) collective-permute-start(f32[2,64,512]{2,1,0:T(8,128)} %add.196), channel_id=1, source_target_pairs={{480,0},{0,32},{32,64},{64,96},{96,128},{128,160},{160,192},{192,2... | collective-permute-start | bytes 786440 | tf_op jit(solution)/shard_map/ppermute | solution.py:14
  630.0 15.8 %collective-permute-start.6 = (bf16[2,64,512]{2,1,0:T(8,128)(2,1)S(1)}, bf16[2,64,512]{2,1,0:T(8,128)(2,1)S(1)}, u32[]{:S(2)}, u32[]{:S(2)}) collective-permute-start(bf16[2,64,512]{2,1,0:T(8,128)(2,1)S(1)} %maximum_add_fusion.2), channel_id=1, source_target_pairs={{480,0},{0,32},{32,64},{64,96},{96,128},{128,160},{160,192},{192,2... | collective-permute-start | bytes 393224 | tf_op jit(solution)/shard_map/ppermute | solution.py:14
  (156 other events, 895.1 us)
where the time goes:
time: 823 us; the launch traced here: 811 us
  starting transfers between devices  189 us (23%)
  waiting for transfers between devices  164 us (20%)
  blocking collectives  164 us (20%)
  local copies, waits for them, and re-layouts  145 us (18%)
  other arithmetic  79.7 us (10%)
  matrix products  62.6 us (8%)
    ppermute x77, starting transfers between devices, from_behind(): return lax.ppermute(block, axis, route)  189 us
    psum x1, blocking collectives, local(): dkv_prompt = lax.psum(accp, 'reply').astype(jnp.bfloat16)  164 us
    ppermute x77, waiting for transfers between devices, from_behind(): return lax.ppermute(block, axis, route)  164 us
    while x300, local copies, waits for them, and re-layouts  84.6 us
    dot_general x18, matrix products, attend(): jnp.einsum('gxqk,kgd->qgxd', dscore_b, k, preferred_element_type=f) * scale  28.4 us
    add x16, other arithmetic, fold_prompt(): return accp + term  27 us
    add x15, other arithmetic, loop_turn(): return (kvp, kvr, maskr, accp, accr, dq_head + dq_one, dq_rows + dq_two)  21.5 us
    another operation x32, local copies, waits for them, and re-layouts  17 us
  transfers between devices with their start and end apart: 77, of which 25 were waited for; matrix products, arithmetic and copies ran while one was open for 29% of the time, Pallas kernels for 0%

commit v1 on v0

v1 whole, which is shorter than its diff:
```python
import jax
import jax.numpy as jnp
from jax import lax
from jax.experimental import pallas as pl
from jax.experimental.pallas import tpu as pltpu
from jax.sharding import PartitionSpec as P

MESH = pl.DeviceIdType.MESH
F32 = jnp.float32
BF16 = jnp.bfloat16
DH = 128
ROWS = 64
HALF = 128
UNIT = 256
WIDE = 1024
SCALE = DH**-0.5
LOG2E = 1.4426950408889634
NN = (((1,), (0,)), ((), ()))
NT = (((1,), (1,)), ((), ()))
TN = (((0,), (0,)), ((), ()))


def dot(a, b, dims=NN):
    return lax.dot_general(a, b, dims, preferred_element_type=F32)


def at(start, size, step):
    return pl.ds(pl.multiple_of(start, step), size)


def kernel(
    qp, dop, kvp, lsep, delp, qr, dor, kvr, lser, delr, rlen, rmask,
    dqp_out, dkvp_out, dqr_out, dkvr_out,
    qbuf, dobuf, qpb, dopb, kpb, krb, lsd_st, lsd_rx, lsp_rx, msk, lse2, del2, rows_p, bias,
    dqa, dqpa, dacc, keep, psend, prx, rsend, rrx, rst, rrcv, ag_st, dq_st, dqp_st, dkv_st,
    loc, qs, qrx, ds, drx, ls, lrx, ps, prs, kp1s, kp1r, kr1s, kr1r, ms1, mr1, kp2s, kp2r, kr2s, kr2r, ms2, mr2,
    pps, ppr, rps, rpr, rss, rsr, ags, agr, os_, or_, fs, fr, dps, dpr,
):
    p = lax.axis_index("prompt")
    r = lax.axis_index("reply")
    y = p // 8
    x = (p // 2) % 4
    c = p % 2
    g = 2 * y + c
    yh = r // 8
    z = r % 8
    handler = r // 8
    turn = (r // 4) % 4
    beyond = 8 * ((yh + 2 * y + 3) % 4) + z
    near = 2 * y + 1 - c

    def device(i, j):
        return 8 * (j // 2) + 2 * i + j % 2

    def mate(j):
        return device(x, j)

    def along(i):
        return 8 * y + 2 * i + c

    def remote(src, dst, send, recv, **where):
        return pltpu.make_async_remote_copy(
            src_ref=src, dst_ref=dst, send_sem=send, recv_sem=recv, device_id=where, device_id_type=MESH
        )

    barrier = pltpu.get_barrier_semaphore()

    def greet(**where):
        pl.semaphore_signal(barrier, inc=1, device_id=where, device_id_type=MESH)

    @pl.loop(1, 4)
    def _(o):
        greet(prompt=mate((g + o) % 4))
        greet(prompt=along((x + o) % 4))

    @pl.loop(0, 2)
    def _(b):
        greet(prompt=mate(2 * (1 - y) + b), reply=beyond)

    @pl.loop(1, 32)
    def _(o):
        greet(reply=(r + o) % 32)

    def giver(i):
        return 16 * (i // 4) + 4 * g + i % 4

    @pl.loop(1, 4)
    def _(o):
        @pl.loop(0, 8)
        def _(i):
            greet(prompt=mate((g + o) % 4), reply=giver(i))

    def group_cols(j):
        return at(DH * j, DH, DH)

    def head_cols(j):
        return at(WIDE * j, WIDE, WIDE)

    def seat(ref, j):
        return ref.at[j // 2, at(ROWS * (j % 2), ROWS, ROWS), :]

    def rows_at(ref, i, j):
        return ref.at[:, at(UNIT * i + ROWS * j, ROWS, ROWS), :]

    def unit_at(ref, i):
        return ref.at[:, at(UNIT * i, UNIT, UNIT), :]

    own_kp = pltpu.make_async_copy(kvp.at[:, :, group_cols(g)], rows_at(kpb, x, g), loc.at[2])
    own_kr = pltpu.make_async_copy(kvr.at[:, 0, :, group_cols(g)], rows_at(krb, x, g), loc.at[3])
    own_q = pltpu.make_async_copy(qr.at[0, :, head_cols(g)], seat(qbuf, g), loc.at[0])
    own_do = pltpu.make_async_copy(dor.at[0, :, head_cols(g)], seat(dobuf, g), loc.at[1])
    own_qp = pltpu.make_async_copy(qp, seat(qpb, g), loc.at[4])
    own_dop = pltpu.make_async_copy(dop, seat(dopb, g), loc.at[5])
    for copy in (own_kp, own_q, own_do, own_kr, own_qp, own_dop):
        copy.start()

    def twice(v):
        return jnp.concatenate([v, v], axis=1)

    for j in range(4):
        lsd_st[j, 0] = twice(lser[0, 8 * j:8 * j + 8, :])
        lsd_st[j, 1] = twice(delr[0, 8 * j:8 * j + 8, :])
    lsp_rx[g, 0:1, :] = twice(lsep[...])
    lsp_rx[g, 1:2, :] = twice(delp[...])
    lsp_rx[g, 2:8, :] = jnp.zeros((6, 128), F32)
    msk[x, g] = jnp.broadcast_to(twice(rmask[...].astype(F32)), (8, 128))
    lsd_rx[g] = lsd_st[g]

    @pl.when(turn == g)
    def _():
        pl.semaphore_wait(barrier, 3 + 3 + 2 + 31)

    @pl.when(turn != g)
    def _():
        pl.semaphore_wait(barrier, 3 + 3 + 2 + 31 + 32)

    def kp1(src, dst, **where):
        piece = kvp.at[:, :, group_cols(dst)]
        return remote(piece, rows_at(kpb, x, src), kp1s.at[dst], kp1r.at[src], prompt=mate(dst), **where)

    def kr1(src, dst):
        return remote(kvr.at[:, 0, :, group_cols(dst)], rows_at(krb, x, src), kr1s.at[dst], kr1r.at[src], prompt=mate(dst))

    def mk1(src, dst):
        return remote(msk.at[x, src], msk.at[x, src], ms1.at[dst], mr1.at[src], prompt=mate(dst))

    def chunk(ref, j, ch):
        return ref.at[j // 2, at(ROWS * (j % 2), ROWS, ROWS), at(512 * ch, 512, 512)]

    def q1(src, dst, ch):
        piece = qr.at[0, :, at(WIDE * dst + 512 * ch, 512, 512)]
        return remote(piece, chunk(qbuf, src, ch), qs.at[dst, ch], qrx.at[src, ch], prompt=mate(dst))

    def do1(src, dst, ch):
        piece = dor.at[0, :, at(WIDE * dst + 512 * ch, 512, 512)]
        return remote(piece, chunk(dobuf, src, ch), ds.at[dst, ch], drx.at[src, ch], prompt=mate(dst))

    def ls1(src, dst):
        return remote(lsd_st.at[dst], lsd_rx.at[src], ls.at[dst], lrx.at[src], prompt=mate(dst))

    def hand(src):
        return [
            remote(qp, seat(qpb, src), ps.at[0], prs.at[0, src], prompt=mate(handler)),
            remote(dop, seat(dopb, src), ps.at[1], prs.at[1, src], prompt=mate(handler)),
            remote(lsp_rx.at[src], lsp_rx.at[src], ps.at[2], prs.at[2, src], prompt=mate(handler)),
        ]

    @pl.loop(0, 2)
    def _(b):
        kp1(g, 2 * (1 - y) + (c + b) % 2, reply=beyond).start()

    kp1(g, near).start()

    ls1(g, near).start()
    for ch in range(2):
        q1(g, near, ch).start()
        do1(g, near, ch).start()

    @pl.loop(0, 2)
    def _(b):
        far = 2 * (1 - y) + (c + b) % 2
        ls1(g, far).start()
        kr1(g, far).start()
        mk1(g, far).start()

    kr1(g, near).start()
    mk1(g, near).start()

    @pl.when(g != handler)
    def _():
        for copy in hand(g):
            copy.start()

    @pl.loop(0, 4)
    def _(b):
        far = 2 * (1 - y) + (c + b) % 2
        q1(g, far, b // 2).start()
        do1(g, far, b // 2).start()

    def kp2(src, dst):
        return remote(unit_at(kpb, src), unit_at(kpb, src), kp2s.at[dst], kp2r.at[src], prompt=along(dst))

    def kr2(src, dst):
        return remote(unit_at(krb, src), unit_at(krb, src), kr2s.at[dst], kr2r.at[src], prompt=along(dst))

    def mk2(src, dst):
        return remote(msk.at[src], msk.at[src], ms2.at[dst], mr2.at[src], prompt=along(dst))

    own_kp.wait()

    @pl.loop(1, 4)
    def _(o):
        kp1((g + o) % 4, g).wait_recv()

    @pl.loop(1, 4)
    def _(o):
        kp2(x, (x + 4 - o) % 4).start()

    dqa[...] = jnp.zeros_like(dqa)
    dacc[...] = jnp.zeros_like(dacc)

    def pass_reply_keys():
        own_kr.wait()

        @pl.loop(1, 4)
        def _(o):
            kr1((g + o) % 4, g).wait_recv()
            mk1((g + o) % 4, g).wait_recv()

        @pl.loop(1, 4)
        def _(o):
            kr2(x, (x + 4 - o) % 4).start()
            mk2(x, (x + 4 - o) % 4).start()

    pass_reply_keys()

    lane = lax.broadcasted_iota(jnp.int32, (1, 128), 1)
    first = lane < 64

    def rows_of(half):
        alive = HALF * x + 512 * half + lane < rlen[0]
        lse = jnp.where(first, lsd_rx[2 * half, 0], lsd_rx[2 * half + 1, 0]) * LOG2E
        lse = jnp.where(alive, lse, jnp.inf)
        delta = jnp.where(first, lsd_rx[2 * half, 1], lsd_rx[2 * half + 1, 1])
        for ch in range(2):
            lse2[half, ch] = jnp.concatenate([lse[h:h + 1] for h in range(4 * ch, 4 * ch + 4)], axis=1)
            del2[half, ch] = jnp.concatenate([delta[h:h + 1] for h in range(4 * ch, 4 * ch + 4)], axis=1)

    own_q.wait()
    own_do.wait()
    for ch in range(2):
        q1(near, g, ch).wait_recv()
        do1(near, g, ch).wait_recv()
    ls1(near, g).wait_recv()
    rows_of(y)

    def heads(ref, half):
        return jnp.concatenate([ref[half, :, DH * h:DH * h + DH] for h in range(8)], axis=0)

    def terms(keys, vals, q, do, lse_row, del_row, add):
        score = dot(keys, q, NT) * (SCALE * LOG2E) - lse_row
        if add is not None:
            score = score + add
        prob = jnp.exp2(score)
        dprob = dot(vals, do, NT)
        prob_b = prob.astype(BF16)
        ds_b = (prob * (dprob - del_row)).astype(BF16)
        return dot(ds_b, keys, TN), dot(ds_b, q), dot(prob_b, do)

    def both(ref, half):
        return jnp.concatenate([ref[half, 0], ref[half, 1]], axis=1)

    def unit(ref, i, half, size, masked):
        rows = at(UNIT * i, size, UNIT)
        add = None
        if masked:
            add = jnp.concatenate([bias[0:size, :]] * 8, axis=1)
        dq, dk, dv = terms(
            ref[0, rows, :], ref[1, rows, :], heads(qbuf, half), heads(dobuf, half), both(lse2, half), both(del2, half), add
        )
        dqa[half] += dq
        dacc[i, 0, 0:size, :] += dk
        dacc[i, 1, 0:size, :] += dv

    def four(ref, half, ch):
        return jnp.concatenate([ref[half, :, at(512 * ch + DH * h, DH, DH)] for h in range(4)], axis=0)

    def unit_chunk(ref, i, half, ch):
        rows = at(UNIT * i, UNIT, UNIT)
        dq, dk, dv = terms(
            ref[0, rows, :], ref[1, rows, :], four(qbuf, half, ch), four(dobuf, half, ch), lse2[half, ch], del2[half, ch], None
        )
        dqa[half, at(512 * ch, 512, 512), :] += dq
        dacc[i, 0] += dk
        dacc[i, 1] += dv

    def causal(i, half, size):
        key = lax.broadcasted_iota(jnp.int32, (HALF, HALF), 0)
        query = lax.broadcasted_iota(jnp.int32, (HALF, HALF), 1)
        return [key - query <= HALF * x + 512 * half - HALF * i - 512 * b for b in range(size // HALF)]

    def set_bias(i, half, size):
        for b, ok in enumerate(causal(i, half, size)):
            row = jnp.where(first, msk[i, 2 * b, 0:1, :], msk[i, 2 * b + 1, 0:1, :])
            column = jnp.transpose(jnp.broadcast_to(row, (HALF, HALF)))
            bias[HALF * b:HALF * b + HALF, :] = jnp.where(ok & (column > 0.5), 0.0, -jnp.inf)

    def partial(buf, rx, send, recv, src, dst):
        return remote(buf.at[dst], rx.at[src], send.at[dst], recv.at[src], prompt=along(dst))

    def finish(buf, rx, send, recv, i):
        @pl.when(i == x)
        def _():
            keep[0] = dacc[x, 0] * SCALE
            keep[1] = dacc[x, 1]

        @pl.when(i != x)
        def _():
            buf[i, 0] = (dacc[i, 0] * SCALE).astype(BF16)
            buf[i, 1] = dacc[i, 1].astype(BF16)
            partial(buf, rx, send, recv, x, i).start()

    def totals_of(buf, rx, send, recv):
        @pl.loop(1, 4)
        def _(o):
            partial(buf, rx, send, recv, (x + o) % 4, x).wait_recv()

        totals = []
        for kv in range(2):
            total = keep[kv]
            for o in range(1, 4):
                total = total + rx[(x + o) % 4, kv].astype(F32)
            totals.append(total.astype(BF16))
        return totals

    @pl.loop(0, 4)
    def _(t):
        i = (x + t) % 4

        @pl.when(t > 0)
        def _():
            kp2(i, x).wait_recv()

        unit(kpb, i, y, UNIT, False)

    @pl.loop(0, 2)
    def _(b):
        ls1(2 * (1 - y) + b, g).wait_recv()

    rows_of(1 - y)

    @pl.when(g == handler)
    def _():
        own_qp.wait()
        own_dop.wait()

        @pl.loop(1, 4)
        def _(o):
            for copy in hand((g + o) % 4):
                copy.wait_recv()

        for b in range(2):
            lse = jnp.where(first, lsp_rx[2 * b, 0:1, :], lsp_rx[2 * b + 1, 0:1, :]) * LOG2E
            delta = jnp.where(first, lsp_rx[2 * b, 1:2, :], lsp_rx[2 * b + 1, 1:2, :])
            rows_p[0:1, DH * b:DH * b + DH] = lse
            rows_p[1:2, DH * b:DH * b + DH] = delta
        dqpa[...] = jnp.zeros_like(dqpa)

        @pl.loop(0, 4)
        def _(i):
            rows = at(UNIT * i, UNIT, UNIT)
            grid = [jnp.concatenate(causal(i, b, UNIT), axis=0) for b in range(2)]
            add = jnp.where(jnp.concatenate(grid, axis=1), 0.0, -jnp.inf)
            dq, dk, dv = terms(
                kpb[0, rows, :], kpb[1, rows, :], qpb[...].reshape(UNIT, DH), dopb[...].reshape(UNIT, DH),
                rows_p[0:1, :], rows_p[1:2, :], add,
            )
            dqpa[...] += dq
            dacc[i, 0] += dk
            dacc[i, 1] += dv

    @pl.loop(0, 8)
    def _(t):
        i = (x + 1 + t) % 4
        ch = t // 4

        @pl.when(t % 4 == 0)
        def _():
            @pl.loop(0, 2)
            def _(b):
                q1(2 * (1 - y) + b, g, ch).wait_recv()
                do1(2 * (1 - y) + b, g, ch).wait_recv()

        unit_chunk(kpb, i, 1 - y, ch)

        @pl.when(t >= 4)
        def _():
            finish(psend, prx, pps, ppr, i)

    def dqp_copy(j):
        return remote(dqp_st.at[j], dqp_out, dps.at[j], dpr.at[0], prompt=mate(j))

    own_dqp = pltpu.make_async_copy(dqp_st.at[g], dqp_out, loc.at[4])

    @pl.when(g == handler)
    def _():
        dqp_st[...] = (dqpa[...] * SCALE).astype(BF16).reshape(4, ROWS, DH)
        own_dqp.start()

        @pl.loop(1, 4)
        def _(o):
            dqp_copy((g + o) % 4).start()

    def r_copy(src, dst):
        return remote(rst.at[dst], rrcv.at[src], rss.at[dst], rsr.at[src], reply=dst)

    def final_piece(kv, i, j):
        return dkvp_out.at[kv, at(16 * i, 16, 16), group_cols(j)]

    def g_send(dst):
        piece = final_piece(r // 16, r % 4, g)
        return remote(ag_st, piece, ags.at[dst], agr.at[g, 4 * (r // 16) + r % 4], prompt=mate(turn), reply=dst)

    def g_recv(j, i):
        return remote(ag_st, final_piece(i // 4, i % 4, j), ags.at[0], agr.at[j, i], prompt=mate(j), reply=giver(i))

    own_g = pltpu.make_async_copy(ag_st, final_piece(r // 16, r % 4, g), loc.at[6])

    def others():
        for far in (2, 1, 3, 0):
            for dz in (4, 3, 5, 2, 6, 1, 7, 0):
                if far or dz:
                    yield 8 * ((r // 8 + far) % 4) + (r + dz) % 8

    def sum_column():
        totals = totals_of(psend, prx, pps, ppr)
        for kv in range(2):
            for i in range(16):
                rst[16 * kv + i] = totals[kv][16 * i:16 * i + 16]

        for other in others():
            r_copy(r, other).start()

    def sum_replies():
        total = rst[r].astype(F32)
        rrcv[r] = jnp.zeros((16, DH), BF16)

        @pl.loop(1, 32)
        def _(o):
            r_copy((r + o) % 32, r).wait_recv()

        for i in range(32):
            total = total + rrcv[i].astype(F32)
        ag_st[...] = total.astype(BF16)

        @pl.when(turn == g)
        def _():
            own_g.start()

        @pl.when(turn != g)
        def _():
            g_send(r).start()

        for other in others():
            g_send(other).start()

    dacc[...] = jnp.zeros_like(dacc)

    def dq_copy(src, dst):
        return remote(dq_st.at[dst], dqr_out.at[0, :, head_cols(src)], os_.at[dst], or_.at[src], prompt=mate(dst))

    own_dq = pltpu.make_async_copy(dq_st.at[g], dqr_out.at[0, :, head_cols(g)], loc.at[0])

    def stage_dq(half):
        part = (dqa[half] * SCALE).astype(BF16)
        for h in range(8):
            for b in range(2):
                dq_st[2 * half + b, :, DH * h:DH * h + DH] = part[HALF * h + ROWS * b:HALF * h + ROWS * b + ROWS]

    @pl.loop(0, 4)
    def _(i):
        @pl.when(i != x)
        def _():
            kr2(i, x).wait_recv()
            mk2(i, x).wait_recv()

        half = (i + 3 - x) // 4
        set_bias(i, half, HALF)
        unit(krb, i, half, HALF, True)

        @pl.when(i > x)
        def _():
            finish(rsend, rrx, rps, rpr, i)

        @pl.when(i == 2)
        def _():
            sum_column()

    stage_dq(0)

    @pl.loop(0, x + 1)
    def _(i):
        set_bias(i, 1, UNIT)
        unit(krb, i, 1, UNIT, True)
        finish(rsend, rrx, rps, rpr, i)

    stage_dq(1)
    own_dq.start()
    dq_copy(g, near).start()
    sum_replies()

    @pl.loop(0, 2)
    def _(b):
        dq_copy(g, 2 * (1 - y) + (c + b) % 2).start()

    totals = totals_of(rsend, rrx, rps, rpr)
    for kv in range(2):
        for j in range(4):
            dkv_st[j, kv] = totals[kv][ROWS * j:ROWS * j + ROWS]

    def f_copy(src, dst):
        return remote(dkv_st.at[dst], dkvr_out.at[:, 0, :, group_cols(src)], fs.at[dst], fr.at[src], prompt=mate(dst))

    own_f = pltpu.make_async_copy(dkv_st.at[g], dkvr_out.at[:, 0, :, group_cols(g)], loc.at[1])
    own_f.start()

    @pl.loop(1, 4)
    def _(o):
        f_copy(g, (g + o) % 4).start()

    own_dq.wait()
    own_f.wait()

    @pl.when(turn == g)
    def _():
        own_g.wait()

    @pl.when(turn != g)
    def _():
        g_send(r).wait_send()

    @pl.when(g == handler)
    def _():
        own_dqp.wait()

        @pl.loop(1, 4)
        def _(o):
            dqp_copy((g + o) % 4).wait_send()

    @pl.when(g != handler)
    def _():
        own_qp.wait()
        own_dop.wait()
        dqp_copy(g).wait_recv()
        for copy in hand(g):
            copy.wait_send()

    @pl.loop(1, 4)
    def _(o):
        other = (g + o) % 4
        dq_copy(other, g).wait_recv()
        kp1(g, other).wait_send()
        kr1(g, other).wait_send()
        mk1(g, other).wait_send()
        for ch in range(2):
            q1(g, other, ch).wait_send()
            do1(g, other, ch).wait_send()
        ls1(g, other).wait_send()
        dq_copy(g, other).wait_send()
        f_copy(other, g).wait_recv()
        f_copy(g, other).wait_send()
        partial(psend, prx, pps, ppr, x, (x + o) % 4).wait_send()
        partial(rsend, rrx, rps, rpr, x, (x + o) % 4).wait_send()
        ring = (x + o) % 4
        kp2(x, ring).wait_send()
        kr2(x, ring).wait_send()
        mk2(x, ring).wait_send()

    @pl.loop(0, 32)
    def _(o):
        j, i = o // 8, o % 8

        @pl.when((j != g) | (giver(i) != r))
        def _():
            g_recv(j, i).wait_recv()

    @pl.loop(1, 32)
    def _(o):
        r_copy(r, (r + o) % 32).wait_send()
        g_send((r + o) % 32).wait_send()


def call(*args):
    anywhere = pl.BlockSpec(memory_space=pl.ANY)
    vmem = pl.BlockSpec(memory_space=pltpu.VMEM)
    smem = pl.BlockSpec(memory_space=pltpu.SMEM)
    dma = pltpu.SemaphoreType.DMA
    out = jax.ShapeDtypeStruct
    four = [dma((4,))] * 2
    pairs = [dma((4, 2))] * 2
    thirtytwo = [dma((32,))] * 2
    results = pl.pallas_call(
        kernel,
        out_shape=(
            pltpu.VMEM((ROWS, DH), BF16),
            pltpu.VMEM((2, ROWS, 512), BF16),
            pltpu.VMEM((1, ROWS, 4096), BF16),
            pltpu.VMEM((2, 1, ROWS, 512), BF16),
        ),
        in_specs=[
            anywhere, anywhere, anywhere, vmem, vmem, anywhere, anywhere, anywhere, vmem, vmem, smem, vmem,
        ],
        out_specs=(vmem, vmem, vmem, vmem),
        scratch_shapes=[
            pltpu.VMEM((2, HALF, WIDE), BF16),
            pltpu.VMEM((2, HALF, WIDE), BF16),
            pltpu.VMEM((2, HALF, DH), BF16),
            pltpu.VMEM((2, HALF, DH), BF16),
            pltpu.VMEM((2, 1024, DH), BF16),
            pltpu.VMEM((2, 1024, DH), BF16),
            pltpu.VMEM((4, 2, 8, 128), F32),
            pltpu.VMEM((4, 2, 8, 128), F32),
            pltpu.VMEM((4, 8, 128), F32),
            pltpu.VMEM((4, 4, 8, 128), F32),
            pltpu.VMEM((2, 2, 1, 512), F32),
            pltpu.VMEM((2, 2, 1, 512), F32),
            pltpu.VMEM((8, UNIT), F32),
            pltpu.VMEM((UNIT, HALF), F32),
            pltpu.VMEM((2, WIDE, DH), F32),
            pltpu.VMEM((UNIT, DH), F32),
            pltpu.VMEM((4, 2, UNIT, DH), F32),
            pltpu.VMEM((2, UNIT, DH), F32),
            pltpu.VMEM((4, 2, UNIT, DH), BF16),
            pltpu.VMEM((4, 2, UNIT, DH), BF16),
            pltpu.VMEM((4, 2, UNIT, DH), BF16),
            pltpu.VMEM((4, 2, UNIT, DH), BF16),
            pltpu.VMEM((32, 16, DH), BF16),
            pltpu.VMEM((32, 16, DH), BF16),
            pltpu.VMEM((16, DH), BF16),
            pltpu.VMEM((4, ROWS, WIDE), BF16),
            pltpu.VMEM((4, ROWS, DH), BF16),
            pltpu.VMEM((4, 2, ROWS, DH), BF16),
            dma((8,)),
            *pairs,
            *pairs,
            *four,
            dma((3,)),
            dma((3, 4)),
            *four,
            *four,
            *four,
            *four,
            *four,
            *four,
            *four,
            *four,
            *thirtytwo,
            dma((32,)),
            dma((4, 8)),
            *four,
            *four,
            *four,
        ],
        compiler_params=pltpu.CompilerParams(
            collective_id=0, has_side_effects=True, vmem_limit_bytes=VMEM_LIMIT
        ),
    )(*args)

    def hand_over(*refs):
        sems = refs[-1]
        copies = [pltpu.make_async_copy(refs[i], refs[4 + i], sems.at[i]) for i in range(4)]
        for copy in copies:
            copy.start()
        for copy in copies:
            copy.wait()

    return pl.pallas_call(
        hand_over,
        out_shape=[out(a.shape, a.dtype) for a in results],
        in_specs=[anywhere] * 4,
        out_specs=[anywhere] * 4,
        scratch_shapes=[dma((4,))],
        compiler_params=pltpu.CompilerParams(vmem_limit_bytes=2**20),
    )(*results)


VMEM_LIMIT = 62 * 2**20


def solution(mesh):
    placed = (
        P("prompt", "reply"),
        P("prompt", "reply"),
        P(None, "prompt", None),
        P("reply", "prompt"),
        P("reply", "prompt"),
        P("reply", "prompt", None),
        P("reply", "prompt", None),
        P(None, "reply", "prompt", None),
        P("reply", None, "prompt"),
        P("reply", None, "prompt"),
        P("reply"),
        P("reply", "prompt"),
    )
    return jax.shard_map(
        call,
        mesh=mesh,
        in_specs=placed,
        out_specs=(
            P("prompt", "reply"),
            P(None, "prompt", None),
            P("reply", "prompt", None),
            P(None, "reply", "prompt", None),
        ),
        check_vma=False,
    )
```

time: 823 us -> 69.1 us (0.08)
  the two profiles are of different devices: /device:TPU:32 before, /device:TPU:1 now
where the time goes in v1:
time: 69.1 us; the launch traced here: 68.9 us
  Pallas kernels  67.6 us (98%)
  between operations  1.29 us (2%)
    pallas_call x1, Pallas kernels, call(): pl.pallas_call(kernel, out_shape=(pltpu.VMEM((ROWS, DH), BF16), pltpu.VME...  66.7 us

profile of v1, /device:TPU:1, one launch (start us, length us, event | category | flops | bytes accessed | tf_op | source)
XLA Modules:
  0.0 68.9 jit_solution(12550509523394776055)
XLA Ops:
  1.3 66.7 %shard_map.147 = (bf16[64,128]{1,0:T(8,128)(2,1)S(1)}, bf16[2,64,512]{2,1,0:T(8,128)(2,1)S(1)}, bf16[1,64,4096]{2,1,0:T(8,128)(2,1)S(1)}, bf16[2,1,64,512]{3,2,1,0:T(8,128)(2,1)S(1)}) custom-call(bf16[64,128]{1,0:T(8,128)(2,1)} %qp.1, bf16[64,128]{1,0:T(8,128)(2,1)} %dop.1, bf16[2,64,512]{2,1,0:T(8,128)(2,1)} %kvp.1, f32[1,64]{1,0:T(1,128)} %lsep.1, ...), custom_call_target="tpu_custom_call" | custom-call | tf_op jit(solution)/shard_map/pallas_call | solution.py:602
  68.0 0.9 %shard_map.148 = (bf16[64,128]{1,0:T(8,128)(2,1)}, bf16[2,64,512]{2,1,0:T(8,128)(2,1)}, bf16[1,64,4096]{2,1,0:T(8,128)(2,1)}, bf16[2,1,64,512]{3,2,1,0:T(8,128)(2,1)}) custom-call(bf16[64,128]{1,0:T(8,128)(2,1)S(1)} %get-tuple-element.8.refs_0_, bf16[2,64,512]{2,1,0:T(8,128)(2,1)S(1)} %get-tuple-element.9.refs_1_, ...), custom_call_target="tpu_custom_call" | custom-call | tf_op jit(solution)/shard_map/pallas_call | solution.py:677
